TPU v7x, 32 devices: a whole 2x2x4 slice. The times are simulated.
32 devices in a mesh: dp: 16 (over z, y, core), tensor: 2 (over x).
Axes of the slice: x: 2, y: 2, z: 4, core: 2. Of those that a mesh axis runs over, the one named last changes fastest.
Arguments:
- tokens: bfloat16 [65536, 1024], P(('dp', 'tensor')), may hold values from -6 to 6
- cotangent: bfloat16 [65536, 1024], P(('dp', 'tensor')), may hold values from -6 to 6
- seq_lengths: int32 [32], replicated, may hold values from 1 to 2048, 40960 in all
- slot_seq: int32 [32], replicated, may hold values from 0 to 31, each once
- w_query: bfloat16 [1024, 1024], P('dp', 'tensor'), may hold values from -0.1875 to 0.1875
- w_key: bfloat16 [1024, 1024], P('dp', 'tensor'), may hold values from -0.1875 to 0.1875
- w_value: bfloat16 [1024, 1024], P('dp', 'tensor'), may hold values from -0.1875 to 0.1875
- b_query: bfloat16 [16, 64], P('tensor', 'dp'), may hold values from -1.5 to 1.5
- b_value: bfloat16 [16, 64], P('tensor', 'dp'), may hold values from -0.25 to 0.25
- w_output: bfloat16 [1024, 1024], P('tensor', 'dp'), may hold values from -2 to 2
- b_output: float32 [1024], P(('dp', 'tensor')), may hold values from -1.5 to 1.5
- gain_first: float32 [1024], P(('dp', 'tensor')), may hold values from 0.1 to 1.9
- shift_first: float32 [1024], P(('dp', 'tensor')), may hold values from -1.5 to 1.5
- w_up: bfloat16 [1024, 4096], P('dp', 'tensor'), may hold values from -0.1875 to 0.1875
- b_up: bfloat16 [64, 64], P('tensor', 'dp'), may hold values from -1.5 to 1.5
- w_down: bfloat16 [4096, 1024], P('tensor', 'dp'), may hold values from -0.09375 to 0.09375
- b_down: float32 [1024], P(('dp', 'tensor')), may hold values from -1.5 to 1.5
- gain_second: float32 [1024], P(('dp', 'tensor')), may hold values from 0.1 to 1.9
- shift_second: float32 [1024], P(('dp', 'tensor')), may hold values from -1.5 to 1.5
Outputs:
- layer_out: float32 [65536, 1024], P(('dp', 'tensor'))
- grad_tokens: float32 [65536, 1024], P(('dp', 'tensor'))
- grad_w_query: float32 [1024, 1024], P('dp', 'tensor')
- grad_w_key: float32 [1024, 1024], P('dp', 'tensor')
- grad_w_value: float32 [1024, 1024], P('dp', 'tensor')
- grad_b_query: float32 [16, 64], P('tensor', 'dp')
- grad_b_value: float32 [16, 64], P('tensor', 'dp')
- grad_w_output: float32 [1024, 1024], P('tensor', 'dp')
- grad_b_output: float32 [1024], P(('dp', 'tensor'))
- grad_gain_first: float32 [1024], P(('dp', 'tensor'))
- grad_shift_first: float32 [1024], P(('dp', 'tensor'))
- grad_w_up: float32 [1024, 4096], P('dp', 'tensor')
- grad_b_up: float32 [64, 64], P('tensor', 'dp')
- grad_w_down: float32 [4096, 1024], P('tensor', 'dp')
- grad_b_down: float32 [1024], P(('dp', 'tensor'))
- grad_gain_second: float32 [1024], P(('dp', 'tensor'))
- grad_shift_second: float32 [1024], P(('dp', 'tensor'))
Inputs may be any that keep to these rules, and one draw needn't show every extreme that they name: `seq_lengths`: the lengths add up to 40960 and the longest is 2048. `slot_seq`: every sequence is in exactly one slot.
All inputs are finite; a program needn't handle non-finite values.
Results may differ from a plain program's by a relative error of at most 0.02.
Values may be sent and summed in bfloat16 or wider, within the bound.
A program may use at most 384 MiB of HBM per device.

v0:
```python
import jax
import jax.numpy as jnp
from jax import lax
from jax.sharding import PartitionSpec as P

HEAD_DIM = 64
SEQ_MAX = 2048


norm_eps = 1e-06
masked_score = -1e30


def matmul(left, right):
    return jnp.dot(left, right, preferred_element_type=jnp.float32)


def contract_rows(left, right):
    return lax.dot_general(
        left, right, (((0,), (0,)), ((), ())), preferred_element_type=jnp.float32
    )


def contract_cols(left, right):
    return lax.dot_general(
        left, right, (((1,), (1,)), ((), ())), preferred_element_type=jnp.float32
    )


def norm_forward(resid, gain, shift):
    center = resid - jnp.mean(resid, axis=-1, keepdims=True)
    inv_std = lax.rsqrt(jnp.mean(center * center, axis=-1, keepdims=True) + norm_eps)
    normal = center * inv_std
    return (normal * gain + shift, normal, inv_std)


def norm_backward(normal, inv_std, gain, upstream):
    scaled = upstream * gain
    mean_one = jnp.mean(scaled, axis=-1, keepdims=True)
    mean_two = jnp.mean(scaled * normal, axis=-1, keepdims=True)
    grad_resid = inv_std * (scaled - mean_one - normal * mean_two)
    return (grad_resid, jnp.sum(upstream * normal, axis=0), jnp.sum(upstream, axis=0))


def masked_scores(query_blk, keys_slot, length, scale):
    scores = (
        jnp.einsum("qhd,khd->hqk", query_blk, keys_slot, preferred_element_type=jnp.float32) * scale
    )
    positions = lax.broadcasted_iota(jnp.int32, scores.shape, 2)
    return jnp.where(positions < length, scores, masked_score)


def attention_forward(queries, keys, values, lengths, scale):
    rows_all = queries.shape[0]
    block_rows = min(512, SEQ_MAX)
    per_slot = SEQ_MAX // block_rows

    def attention_one_block(block_index):
        slot_index = block_index // per_slot
        query_blk = lax.dynamic_slice_in_dim(queries, block_index * block_rows, block_rows, 0)
        keys_slot = lax.dynamic_slice_in_dim(keys, slot_index * SEQ_MAX, SEQ_MAX, 0)
        values_slot = lax.dynamic_slice_in_dim(values, slot_index * SEQ_MAX, SEQ_MAX, 0)
        length = lax.dynamic_index_in_dim(lengths, slot_index, 0, keepdims=False)
        scores = masked_scores(query_blk, keys_slot, length, scale)
        row_peak = jnp.max(scores, axis=-1, keepdims=True)
        exponent = jnp.exp(scores - row_peak)
        summed = jnp.sum(exponent, axis=-1, keepdims=True)
        attn_probs = (exponent / summed).astype(jnp.bfloat16)
        attended = jnp.einsum(
            "hqk,khd->qhd", attn_probs, values_slot, preferred_element_type=jnp.float32
        )
        return (attended, (row_peak + jnp.log(summed))[..., 0])

    block_ids = jnp.arange(rows_all // block_rows, dtype=jnp.int32)
    attended, log_sums = lax.map(attention_one_block, block_ids)
    return (attended.reshape(rows_all, -1), log_sums)


def attention_backward(queries, keys, values, lengths, log_sums, grad_out, scale):
    rows_all = queries.shape[0]
    block_rows = min(512, SEQ_MAX)
    per_slot = SEQ_MAX // block_rows

    def one_slot(slot_index):
        keys_slot = lax.dynamic_slice_in_dim(keys, slot_index * SEQ_MAX, SEQ_MAX, 0)
        values_slot = lax.dynamic_slice_in_dim(values, slot_index * SEQ_MAX, SEQ_MAX, 0)
        length = lax.dynamic_index_in_dim(lengths, slot_index, 0, keepdims=False)

        def one_one_block(carried, block_index):
            grad_keys, grad_values = carried
            row_start = slot_index * SEQ_MAX + block_index * block_rows
            query_blk = lax.dynamic_slice_in_dim(queries, row_start, block_rows, 0)
            grad_blk = lax.dynamic_slice_in_dim(grad_out, row_start, block_rows, 0)
            lse_blk = lax.dynamic_index_in_dim(
                log_sums, slot_index * per_slot + block_index, 0, keepdims=False
            )
            scores = masked_scores(query_blk, keys_slot, length, scale)
            attn_probs = jnp.exp(scores - lse_blk[..., None])
            grad_values = grad_values + jnp.einsum(
                "hqk,qhd->khd",
                attn_probs.astype(jnp.bfloat16),
                grad_blk,
                preferred_element_type=jnp.float32,
            )
            grad_probs = jnp.einsum(
                "qhd,khd->hqk", grad_blk, values_slot, preferred_element_type=jnp.float32
            )
            inner = jnp.sum(attn_probs * grad_probs, axis=-1, keepdims=True)
            grad_scores = (attn_probs * (grad_probs - inner)).astype(jnp.bfloat16)
            grad_query = (
                jnp.einsum(
                    "hqk,khd->qhd", grad_scores, keys_slot, preferred_element_type=jnp.float32
                )
                * scale
            )
            grad_keys = (
                grad_keys
                + jnp.einsum(
                    "hqk,qhd->khd", grad_scores, query_blk, preferred_element_type=jnp.float32
                )
                * scale
            )
            return ((grad_keys, grad_values), grad_query)

        zero_slot = jnp.zeros(keys_slot.shape, jnp.float32)
        (grad_keys, grad_values), grad_queries = lax.scan(
            one_one_block, (zero_slot, zero_slot), jnp.arange(per_slot, dtype=jnp.int32)
        )
        return (grad_queries.reshape(keys_slot.shape), grad_keys, grad_values)

    slot_ids = jnp.arange(rows_all // SEQ_MAX, dtype=jnp.int32)
    grad_q, grad_k, grad_v = lax.map(one_slot, slot_ids)
    width = queries.shape[1] * queries.shape[2]
    return (
        grad_q.reshape(rows_all, width).astype(jnp.bfloat16),
        grad_k.reshape(rows_all, width).astype(jnp.bfloat16),
        grad_v.reshape(rows_all, width).astype(jnp.bfloat16),
    )


def per_device(
    tokens,
    cotangent,
    seq_lengths,
    slot_seq,
    w_query,
    w_key,
    w_value,
    b_query,
    b_value,
    w_output,
    b_output,
    gain_first,
    shift_first,
    w_up,
    b_up,
    w_down,
    b_down,
    gain_second,
    shift_second,
):
    local_rows = tokens.shape[0]
    group_rows = local_rows * lax.axis_size("tensor")
    slot_count = group_rows // SEQ_MAX
    group_index = lax.axis_index("dp")
    my_slots = lax.dynamic_slice_in_dim(slot_seq, group_index * slot_count, slot_count, 0)
    seq_ids = jnp.arange(seq_lengths.shape[0], dtype=jnp.int32)
    lengths = jnp.sum(
        jnp.where(my_slots[:, None] == seq_ids[None, :], seq_lengths[None, :], 0), axis=1
    )
    scale = HEAD_DIM ** (-0.5)
    (
        query_full,
        key_full,
        value_full,
        bias_query,
        bias_value,
        out_rows,
        up_full,
        bias_up,
        down_full,
    ) = (
        lax.all_gather(w_query, "dp", axis=0, tiled=True),
        lax.all_gather(w_key, "dp", axis=0, tiled=True),
        lax.all_gather(w_value, "dp", axis=0, tiled=True),
        lax.all_gather(b_query, "dp", axis=1, tiled=True),
        lax.all_gather(b_value, "dp", axis=1, tiled=True),
        lax.all_gather(w_output, "dp", axis=1, tiled=True),
        lax.all_gather(w_up, "dp", axis=0, tiled=True),
        lax.all_gather(b_up, "dp", axis=1, tiled=True),
        lax.all_gather(w_down, "dp", axis=1, tiled=True),
    )
    bias_out, bias_down, gain_one, shift_one, gain_two, shift_two = (
        lax.all_gather(b_output, ("dp", "tensor"), axis=0, tiled=True),
        lax.all_gather(b_down, ("dp", "tensor"), axis=0, tiled=True),
        lax.all_gather(gain_first, ("dp", "tensor"), axis=0, tiled=True),
        lax.all_gather(shift_first, ("dp", "tensor"), axis=0, tiled=True),
        lax.all_gather(gain_second, ("dp", "tensor"), axis=0, tiled=True),
        lax.all_gather(shift_second, ("dp", "tensor"), axis=0, tiled=True),
    )
    tokens_all = lax.all_gather(tokens, "tensor", axis=0, tiled=True)
    queries = (matmul(tokens_all, query_full) + bias_query.reshape(-1).astype(jnp.float32)).astype(
        jnp.bfloat16
    )
    keys = matmul(tokens_all, key_full).astype(jnp.bfloat16)
    values = (matmul(tokens_all, value_full) + bias_value.reshape(-1).astype(jnp.float32)).astype(
        jnp.bfloat16
    )
    heads_local = queries.shape[1] // HEAD_DIM
    shape_three = (group_rows, heads_local, HEAD_DIM)
    queries_three = queries.reshape(shape_three)
    keys_three = keys.reshape(shape_three)
    values_three = values.reshape(shape_three)
    attended, log_sums = attention_forward(queries_three, keys_three, values_three, lengths, scale)
    mixed = attended.astype(jnp.bfloat16)
    branch = lax.psum_scatter(matmul(mixed, out_rows), "tensor", scatter_dimension=0, tiled=True)
    resid_one = tokens.astype(jnp.float32) + (branch + bias_out)
    normed, normal_one, inv_one = norm_forward(resid_one, gain_one, shift_one)
    normed_all = lax.all_gather(normed.astype(jnp.bfloat16), "tensor", axis=0, tiled=True)
    hidden_pre = matmul(normed_all, up_full) + bias_up.reshape(-1).astype(jnp.float32)
    hidden = jax.nn.gelu(hidden_pre, approximate=False).astype(jnp.bfloat16)
    second = lax.psum_scatter(
        matmul(hidden, down_full).astype(jnp.bfloat16), "tensor", scatter_dimension=0, tiled=True
    ).astype(jnp.float32)
    resid_two = normed + (second + bias_down)
    layer_out, normal_two, inv_two = norm_forward(resid_two, gain_two, shift_two)
    grad_two, grad_gain_two, grad_shift_two = norm_backward(
        normal_two, inv_two, gain_two, cotangent.astype(jnp.float32)
    )
    grad_second = grad_two.astype(jnp.bfloat16)
    grad_bias_down = jnp.sum(grad_second, axis=0, dtype=jnp.float32)
    grad_second_all = lax.all_gather(grad_second, "tensor", axis=0, tiled=True)
    grad_down = contract_rows(hidden, grad_second_all)
    grad_hidden = contract_cols(grad_second_all, down_full)
    gelu_value, gelu_pull = jax.vjp(
        lambda pre_act: jax.nn.gelu(pre_act, approximate=False), hidden_pre
    )
    grad_pre = gelu_pull(grad_hidden)[0].astype(jnp.bfloat16)
    grad_upw = contract_rows(normed_all, grad_pre)
    grad_bias_up = jnp.sum(grad_pre, axis=0, dtype=jnp.float32).reshape(-1, HEAD_DIM)
    grad_normed = grad_two + lax.psum_scatter(
        contract_cols(grad_pre, up_full), "tensor", scatter_dimension=0, tiled=True
    )
    grad_one, grad_gain_one, grad_shift_one = norm_backward(
        normal_one, inv_one, gain_one, grad_normed
    )
    grad_branch = grad_one.astype(jnp.bfloat16)
    grad_bias_out = jnp.sum(grad_branch, axis=0, dtype=jnp.float32)
    grad_branch_all = lax.all_gather(grad_branch, "tensor", axis=0, tiled=True)
    grad_outw = contract_rows(mixed, grad_branch_all)
    grad_mixed = contract_cols(grad_branch_all, out_rows).astype(jnp.bfloat16)
    grad_queries, grad_keys, grad_values = attention_backward(
        queries_three,
        keys_three,
        values_three,
        lengths,
        log_sums,
        grad_mixed.reshape(shape_three),
        scale,
    )
    grad_queryw = contract_rows(tokens_all, grad_queries)
    grad_keyw = contract_rows(tokens_all, grad_keys)
    grad_valuew = contract_rows(tokens_all, grad_values)
    grad_bias_query = jnp.sum(grad_queries, axis=0, dtype=jnp.float32).reshape(
        heads_local, HEAD_DIM
    )
    grad_bias_value = jnp.sum(grad_values, axis=0, dtype=jnp.float32).reshape(heads_local, HEAD_DIM)
    query_part = contract_cols(grad_queries, query_full)
    key_part = contract_cols(grad_keys, key_full)
    value_part = contract_cols(grad_values, value_full)
    grad_tokens = grad_one + lax.psum_scatter(
        (query_part + key_part + value_part).astype(jnp.bfloat16),
        "tensor",
        scatter_dimension=0,
        tiled=True,
    ).astype(jnp.float32)
    out_wq, out_wk, out_wv, out_bq, out_bv, out_wo, out_wup, out_bup, out_wdown = (
        lax.psum_scatter(
            grad_queryw.astype(jnp.bfloat16), "dp", scatter_dimension=0, tiled=True
        ).astype(jnp.float32),
        lax.psum_scatter(
            grad_keyw.astype(jnp.bfloat16), "dp", scatter_dimension=0, tiled=True
        ).astype(jnp.float32),
        lax.psum_scatter(
            grad_valuew.astype(jnp.bfloat16), "dp", scatter_dimension=0, tiled=True
        ).astype(jnp.float32),
        lax.psum_scatter(
            grad_bias_query.astype(jnp.bfloat16), "dp", scatter_dimension=1, tiled=True
        ).astype(jnp.float32),
        lax.psum_scatter(
            grad_bias_value.astype(jnp.bfloat16), "dp", scatter_dimension=1, tiled=True
        ).astype(jnp.float32),
        lax.psum_scatter(
            grad_outw.astype(jnp.bfloat16), "dp", scatter_dimension=1, tiled=True
        ).astype(jnp.float32),
        lax.psum_scatter(
            grad_upw.astype(jnp.bfloat16), "dp", scatter_dimension=0, tiled=True
        ).astype(jnp.float32),
        lax.psum_scatter(
            grad_bias_up.astype(jnp.bfloat16), "dp", scatter_dimension=1, tiled=True
        ).astype(jnp.float32),
        lax.psum_scatter(
            grad_down.astype(jnp.bfloat16), "dp", scatter_dimension=1, tiled=True
        ).astype(jnp.float32),
    )
    out_bo, out_bdown, out_gain_one, out_shift_one, out_gain_two, out_shift_two = (
        lax.psum_scatter(grad_bias_out, ("dp", "tensor"), scatter_dimension=0, tiled=True),
        lax.psum_scatter(grad_bias_down, ("dp", "tensor"), scatter_dimension=0, tiled=True),
        lax.psum_scatter(grad_gain_one, ("dp", "tensor"), scatter_dimension=0, tiled=True),
        lax.psum_scatter(grad_shift_one, ("dp", "tensor"), scatter_dimension=0, tiled=True),
        lax.psum_scatter(grad_gain_two, ("dp", "tensor"), scatter_dimension=0, tiled=True),
        lax.psum_scatter(grad_shift_two, ("dp", "tensor"), scatter_dimension=0, tiled=True),
    )
    return (
        layer_out,
        grad_tokens,
        out_wq,
        out_wk,
        out_wv,
        out_bq,
        out_bv,
        out_wo,
        out_bo,
        out_gain_one,
        out_shift_one,
        out_wup,
        out_bup,
        out_wdown,
        out_bdown,
        out_gain_two,
        out_shift_two,
    )


def solution(mesh):
    in_specs = (
        P(("dp", "tensor"), None),
        P(("dp", "tensor"), None),
        P(),
        P(),
        P("dp", "tensor"),
        P("dp", "tensor"),
        P("dp", "tensor"),
        P("tensor", "dp"),
        P("tensor", "dp"),
        P("tensor", "dp"),
        P(("dp", "tensor")),
        P(("dp", "tensor")),
        P(("dp", "tensor")),
        P("dp", "tensor"),
        P("tensor", "dp"),
        P("tensor", "dp"),
        P(("dp", "tensor")),
        P(("dp", "tensor")),
        P(("dp", "tensor")),
    )
    out_specs = (
        P(("dp", "tensor"), None),
        P(("dp", "tensor"), None),
        P("dp", "tensor"),
        P("dp", "tensor"),
        P("dp", "tensor"),
        P("tensor", "dp"),
        P("tensor", "dp"),
        P("tensor", "dp"),
        P(("dp", "tensor")),
        P(("dp", "tensor")),
        P(("dp", "tensor")),
        P("dp", "tensor"),
        P("tensor", "dp"),
        P("tensor", "dp"),
        P(("dp", "tensor")),
        P(("dp", "tensor")),
        P(("dp", "tensor")),
    )
    return jax.shard_map(
        per_device, mesh=mesh, in_specs=in_specs, out_specs=out_specs, check_vma=False
    )
```

profile of v0, /device:TPU:0, one launch (start us, length us, event | category | flops | bytes accessed | tf_op | source)
XLA Modules:
  0.0 3045.5 jit_solution(15962512770861209364)
XLA Ops:
  53.6 101.8 %all-gather.14.cloned.1.call-done = bf16[4096,1024]{1,0:T(8,128)(2,1)} async-done(((bf16[2048,1024]{1,0:T(8,128)(2,1)}), bf16[4096,1024]{1,0:T(8,128)(2,1)}) %all-gather.14.cloned.1.call-update) | async-done | bytes 8388624 | tf_op jit(solution)/shard_map/all_gather | solution.py:201
  165.6 30.0 all-gather.16.cloned.1.call-done
  205.7 28.8 all-gather.18.cloned.1.call-done
  244.8 406.6 %while.45 = (s32[]{:T(128)}, bf16[8,512,8,64]{1,3,2,0:T(8,128)(2,1)}, f32[8,8,512]{2,1,0:T(8,128)}, s32[8]{0:T(128)S(1)}, bf16[4096,8,64]{0,2,1:T(8,128)(2,1)}, ...) while((s32[]{:T(128)}, ...), condition=%wide.region_4.5_spmd, body=%wide.region_1.4_spmd.sunk | while | flops 2248144896 | bytes 106570216 | solution.py:75
  675.2 40.2 %all-reduce.16 = (f32[1024]{0:T(1024)S(1)}, f32[1024]{0:T(1024)S(1)}, f32[1024]{0:T(1024)S(1)}, f32[1024]{0:T(1024)}, f32[1024]{0:T(1024)}) all-reduce(f32[1024]{0:T(1024)S(1)} %dynamic-update-slice, f32[1024]{0:T(1024)S(1)} %dynamic-update-slice.2, f32[1024]{0:T(1024)S(1)} %dynamic-update-slice.1, ...), channel_id=1, replica_groups=mesh['dp'=16,'tensor'=2] {'dp','tensor'}, use_global_device_ids=true, to_apply=%add | all-reduce | flops 5120 | bytes 40960
  715.4 147.4 %reduce-scatter.18.cloned.1.call-done = f32[2048,1024]{1,0:T(8,128)} async-done(((f32[4096,1024]{1,0:T(8,128)}), f32[2048,1024]{1,0:T(8,128)}) %reduce-scatter.18.cloned.1.call-update) | async-done | bytes 8388624 | tf_op jit(solution)/shard_map/reduce_scatter | solution.py:216
  915.8 104.7 %all-gather.24.cloned.1.call-done = bf16[4096,1024]{1,0:T(8,128)(2,1)} async-done(((bf16[2048,1024]{1,0:T(8,128)(2,1)}), bf16[4096,1024]{1,0:T(8,128)(2,1)}) %all-gather.24.cloned.1.call-update) | async-done | bytes 8388624 | tf_op jit(solution)/shard_map/all_gather | solution.py:219
  1020.5 93.7 %multiply_convert_fusion.1 = (bf16[4096,2048]{1,0:T(8,128)(2,1)}, f32[4096,2048]{1,0:T(8,128)}, f32[4096,2048]{1,0:T(8,128)}) fusion(f32[2048]{0:T(1024)S(1)} %reshape.174, bf16[4096,1024]{1,0:T(8,128)(2,1)} %all-gather.24.cloned.1.call-done, bf16[1024,2048]{1,0:T(8,128)(2,1)} %all-gather.26.cloned.1.call-done), kind=kOutput, calls=%fused_computation.47 | convolution fusion | flops 17733517312 | bytes 96477184 | tf_op jit(solution)/shard_map/dot_general | solution.py:15
  1138.0 99.3 %reduce-scatter.20.cloned.1.call-done = bf16[2048,1024]{1,0:T(8,128)(2,1)} async-done(((bf16[4096,1024]{1,0:T(8,128)(2,1)}), bf16[2048,1024]{1,0:T(8,128)(2,1)}) %reduce-scatter.20.cloned.1.call-update) | async-done | bytes 4194320 | tf_op jit(solution)/shard_map/reduce_scatter | solution.py:222
  1257.8 104.1 %all-gather.30.cloned.1.call-done = bf16[4096,1024]{1,0:T(8,128)(2,1)} async-done(((bf16[2048,1024]{1,0:T(8,128)(2,1)}), bf16[4096,1024]{1,0:T(8,128)(2,1)}) %all-gather.30.cloned.1.call-update) | async-done | bytes 8388624 | tf_op jit(solution)/shard_map/all_gather | solution.py:232
  1361.9 41.9 %fusion.57 = (bf16[2048]{0:T(1024)(128)(2,1)}, bf16[4096,2048]{1,0:T(8,128)(2,1)}) fusion(f32[4096,2048]{1,0:T(8,128)} %get-tuple-element.579, bf16[4096,1024]{1,0:T(8,128)(2,1)} %all-gather.30.cloned.1.call-done, bf16[2048,1024]{0,1:T(8,128)(2,1)} %all-gather.28.cloned.1.call-done, f32[4096,2048]{1,0:T(8,128)} %get-tuple-element.588, f32[2048]{0:T(1024)S(1)} %reshape.174), kind=kOutput, calls=%fused_computation.119 | convolution fusion | flops 17314084864 | bytes 96481280 | tf_op jit(solution)/shard_map/dot_general | solution.py:25
  1427.5 189.2 %reduce-scatter.22.cloned.1.call-done = f32[2048,1024]{1,0:T(8,128)} async-done(((f32[4096,1024]{1,0:T(8,128)}), f32[2048,1024]{1,0:T(8,128)}) %reduce-scatter.22.cloned.1.call-update) | async-done | bytes 8388624 | tf_op jit(solution)/shard_map/reduce_scatter | solution.py:241
  1688.2 56.1 %all-gather.32.cloned.1.call-done = bf16[4096,1024]{1,0:T(8,128)(2,1)} async-done(((bf16[2048,1024]{1,0:T(8,128)(2,1)}), bf16[4096,1024]{1,0:T(8,128)(2,1)}) %all-gather.32.cloned.1.call-update) | async-done | bytes 8388624 | tf_op jit(solution)/shard_map/all_gather | solution.py:249
  1753.8 884.7 %while.47 = (s32[]{:T(128)}, bf16[2,2048,8,64]{3,2,1,0:T(8,128)(2,1)}, bf16[2,2048,8,64]{1,3,2,0:T(8,128)(2,1)}, bf16[2,2048,8,64]{1,3,2,0:T(8,128)(2,1)}, s32[2...) while((s32[]{:T(128)}, ...), condition=%wide.region_20.21_spmd, body=%wide.region_16.20_spmd.sunk | while | flops 5449709568 | bytes 424760448 | solution.py:132
  1763.6 419.9 %while.48 = (s32[]{:T(128)}, f32[2048,8,64]{0,2,1:T(8,128)}, f32[2048,8,64]{0,2,1:T(8,128)}, bf16[4,512,8,64]{1,3,2,0:T(8,128)(2,1)}, s32[4]{0:T(128)S(1)}, /*in...) while((s32[]{:T(128)}, f32[2048,8,64]{0,2,1:T(8,128)}, ...), condition=%wide.region_19.19_spmd.clone, body=%wide.region_17.18_spmd.clone.sunk | while | flops 5449709568 | bytes 353456512 | solution.py:126
  1805.8 28.1 multiply_convert_fusion.3
  1911.0 27.4 multiply_convert_fusion.3
  2015.7 27.4 multiply_convert_fusion.3
  2120.4 27.4 multiply_convert_fusion.3
  2207.4 416.3 %while.48 = (s32[]{:T(128)}, f32[2048,8,64]{0,2,1:T(8,128)}, f32[2048,8,64]{0,2,1:T(8,128)}, bf16[4,512,8,64]{1,3,2,0:T(8,128)(2,1)}, s32[4]{0:T(128)S(1)}, /*in...) while((s32[]{:T(128)}, f32[2048,8,64]{0,2,1:T(8,128)}, ...), condition=%wide.region_19.19_spmd.clone, body=%wide.region_17.18_spmd.clone.sunk | while | flops 5449709568 | bytes 353456512 | solution.py:126
  2764.4 40.4 %all-reduce.15 = (f32[1024]{0:T(1024)S(1)}, f32[1024]{0:T(1024)S(1)}, f32[1024]{0:T(1024)S(1)}, f32[1024]{0:T(1024)S(1)}, f32[1024]{0:T(1024)S(1)}, /*index=5*/f32[1024]{0:T(1024)S(1)}, f32[1024]{0:T(1024)S(1)}) all-reduce(f32[1024]{0:T(1024)S(1)} %dynamic-update-slice.5, ...), channel_id=1, replica_groups=mesh['dp'=16,'tensor'=2] {'dp','tensor'}, use_global_device_ids=true, to_apply=%add.5 | all-reduce | flops 7168 | bytes 57344
  2824.3 60.1 %all-reduce.17 = (bf16[8,64]{0,1:T(8,128)(2,1)S(1)}, bf16[8,64]{0,1:T(8,128)(2,1)S(1)}, bf16[32,64]{1,0:T(8,128)(2,1)S(1)}) all-reduce(bf16[8,64]{0,1:T(8,128)(2,1)S(1)} %copy.82, bf16[8,64]{0,1:T(8,128)(2,1)S(1)} %copy.83, bf16[32,64]{1,0:T(8,128)(2,1)S(1)} %convert_element_type.233), channel_id=9, replica_groups=mesh['dp'=16,'tensor'=2] {'dp'}, use_global_device_ids=true, to_apply=%region_26.27.clone | all-reduce | flops 3072 | bytes 12288
  2891.4 36.3 %reduce-scatter.26.cloned.1.call-done = bf16[512,64]{0,1:T(8,128)(2,1)} async-done(((bf16[512,1024]{0,1:T(8,128)(2,1)}), bf16[512,64]{0,1:T(8,128)(2,1)}) %reduce-scatter.26.cloned.1.call-update) | async-done | bytes 65552 | tf_op jit(solution)/shard_map/reduce_scatter | solution.py:293
  2929.2 99.0 %reduce-scatter.24.cloned.1.call-done = bf16[2048,1024]{1,0:T(8,128)(2,1)} async-done(((bf16[4096,1024]{1,0:T(8,128)(2,1)}), bf16[2048,1024]{1,0:T(8,128)(2,1)}) %reduce-scatter.24.cloned.1.call-update) | async-done | bytes 4194320 | tf_op jit(solution)/shard_map/reduce_scatter | solution.py:271
  (428 shorter events, 1602.3 us)
Async XLA Ops:
  7.2 46.4 %all-gather.20.cloned.1.call-start = ((), (), s32[]{:S(2)}) async-start(), calls=%async_computation.13 | async-start | bytes 1114112 | tf_op jit(solution)/shard_map/all_gather | solution.py:184
  7.9 147.4 %all-gather.14.cloned.1.call-start = ((), (), s32[]{:S(2)}) async-start(), calls=%async_computation.10 | async-start | bytes 12582912 | tf_op jit(solution)/shard_map/all_gather | solution.py:201
  8.7 186.8 %all-gather.16.cloned.1.call-start = ((), (), s32[]{:S(2)}) async-start(), calls=%async_computation.11 | async-start | bytes 1114112 | tf_op jit(solution)/shard_map/all_gather | solution.py:185
  9.4 225.0 %all-gather.18.cloned.1.call-start = ((), (), s32[]{:S(2)}) async-start(), calls=%async_computation.12 | async-start | bytes 1114112 | tf_op jit(solution)/shard_map/all_gather | solution.py:183
  10.0 650.3 %all-gather.22.cloned.1.call-start = ((), (), s32[]{:S(2)}) async-start(), calls=%async_computation.14 | async-start | bytes 1114112 | tf_op jit(solution)/shard_map/all_gather | solution.py:188
  10.6 852.2 %reduce-scatter.18.cloned.1.call-start = ((), (), s32[]{:S(2)}) async-start(), calls=%async_computation.15 | async-start | bytes 25165824 | tf_op jit(solution)/shard_map/reduce_scatter | solution.py:216
  673.2 242.6 %all-gather.26.cloned.1.call-start = ((), (), s32[]{:S(2)}) async-start(), calls=%async_computation.17 | async-start | bytes 4456448 | tf_op jit(solution)/shard_map/all_gather | solution.py:189
  673.9 346.6 %all-gather.24.cloned.1.call-start = ((), (), s32[]{:S(2)}) async-start(), calls=%async_computation.16 | async-start | bytes 12582912 | tf_op jit(solution)/shard_map/all_gather | solution.py:219
  715.4 154.4 %copy-start.20 = (f32[1024]{0:T(1024)}, f32[1024]{0:T(1024)S(1)}, u32[]{:S(2)}) copy-start(f32[1024]{0:T(1024)S(1)} %get-tuple-element.564) | copy-start | bytes 12292
  715.4 154.4 %copy-start.27 = (f32[1024]{0:T(1024)}, f32[1024]{0:T(1024)S(1)}, u32[]{:S(2)}) copy-start(f32[1024]{0:T(1024)S(1)} %get-tuple-element.563) | copy-start | bytes 12292
  874.8 239.5 %all-gather.28.cloned.1.call-start = ((), (), s32[]{:S(2)}) async-start(), calls=%async_computation.18 | async-start | bytes 4456448 | tf_op jit(solution)/shard_map/all_gather | solution.py:191
  875.5 361.9 %reduce-scatter.20.cloned.1.call-start = ((), (), s32[]{:S(2)}) async-start(), calls=%async_computation.19 | async-start | bytes 12582912 | tf_op jit(solution)/shard_map/reduce_scatter | solution.py:222
  1138.0 224.0 %all-gather.30.cloned.1.call-start = ((), (), s32[]{:S(2)}) async-start(), calls=%async_computation.20 | async-start | bytes 12582912 | tf_op jit(solution)/shard_map/all_gather | solution.py:232
  1243.5 373.2 %copy-start.10 = (f32[2048]{0:T(1024)}, f32[2048]{0:T(1024)S(1)}, u32[]{:S(2)}) copy-start(f32[2048]{0:T(1024)S(1)} %broadcast_multiply_fusion.4) | copy-start | bytes 24580
  1244.7 372.0 %copy-start.14 = (f32[2048]{0:T(1024)}, f32[2048]{0:T(1024)S(1)}, u32[]{:S(2)}) copy-start(f32[2048]{0:T(1024)S(1)} %add_rsqrt_fusion) | copy-start | bytes 24580
  1257.8 358.9 %reduce-scatter.22.cloned.1.call-start = ((), (), s32[]{:S(2)}) async-start(), calls=%async_computation.21 | async-start | bytes 25165824 | tf_op jit(solution)/shard_map/reduce_scatter | solution.py:241
  1427.4 316.9 %all-gather.32.cloned.1.call-start = ((), (), s32[]{:S(2)}) async-start(), calls=%async_computation.22 | async-start | bytes 12582912 | tf_op jit(solution)/shard_map/all_gather | solution.py:249
  1640.1 1120.7 %reduce-scatter.30.cloned.1.call-start = ((), (), s32[]{:S(2)}) async-start(), calls=%async_computation.26 | async-start | bytes 4456448 | tf_op jit(solution)/shard_map/reduce_scatter | solution.py:302
  1664.1 1098.5 %reduce-scatter.28.cloned.1.call-start = ((), (), s32[]{:S(2)}) async-start(), calls=%async_computation.25 | async-start | bytes 4456448 | tf_op jit(solution)/shard_map/reduce_scatter | solution.py:296
  1688.1 1198.1 %reduce-scatter.32.cloned.1.call-start = ((), (), s32[]{:S(2)}) async-start(), calls=%async_computation.27 | async-start | bytes 1114112
  2689.3 198.7 %reduce-scatter.34.cloned.1.call-start = ((), (), s32[]{:S(2)}) async-start(), calls=%async_computation.28 | async-start | bytes 1114112
  2699.8 189.9 %reduce-scatter.36.cloned.1.call-start = ((), (), s32[]{:S(2)}) async-start(), calls=%async_computation.29 | async-start | bytes 1114112
  2710.8 216.9 %reduce-scatter.26.cloned.1.call-start = ((), (), s32[]{:S(2)}) async-start(), calls=%async_computation.24 | async-start | bytes 1114112 | tf_op jit(solution)/shard_map/reduce_scatter | solution.py:293
  2721.1 307.2 %reduce-scatter.24.cloned.1.call-start = ((), (), s32[]{:S(2)}) async-start(), calls=%async_computation.23 | async-start | bytes 12582912 | tf_op jit(solution)/shard_map/reduce_scatter | solution.py:271
  (63 other events, 1194.3 us)
Sparse Core Ops, SparseCore 0:
  10.2 40.6 all-gather.19
  52.4 102.9 all-gather.13
  157.5 37.9 all-gather.15
  197.5 36.8 all-gather.17
  236.4 36.8 all-gather.21
  673.3 189.4 reduce-scatter.17
  865.2 50.5 all-gather.25
  918.0 102.4 all-gather.23
  1022.9 50.7 all-gather.27
  1138.1 99.2 reduce-scatter.19
  1257.9 103.9 all-gather.29
  1427.5 189.1 reduce-scatter.21
  1640.2 104.0 all-gather.31
  1748.5 72.4 reduce-scatter.29
  1824.7 71.3 reduce-scatter.27
  2689.4 57.5 reduce-scatter.31
  2750.4 56.5 reduce-scatter.33
  2811.0 56.5 reduce-scatter.35
  2871.2 56.5 reduce-scatter.25
  2930.0 98.2 reduce-scatter.23
where the time goes:
time: 3060 us; the launch traced here: 3050 us
  matrix products  1180 us (39%)
  waiting for transfers between devices  1020 us (33%)
  other arithmetic  433 us (14%)
  blocking collectives  203 us (7%)
  local copies, waits for them, and re-layouts  143 us (5%)
  loops' own time  43.9 us (1%)
    dot_general x16, matrix products, masked_scores(): jnp.einsum('qhd,khd->hqk', query_blk, keys_slot, preferred_element_type=j...  309 us
    convert_element_type x8, other arithmetic, one_one_block(): grad_scores = (attn_probs * (grad_probs - inner)).astype(jnp.bfloat16)  220 us
    reduce_scatter x1, waiting for transfers between devices, per_device(): lax.psum_scatter(contract_cols(grad_pre, up_full), 'tensor', scatter_dime...  189 us
    dot_general x6, matrix products, matmul(): return jnp.dot(left, right, preferred_element_type=jnp.float32)  161 us
    reduce_scatter x1, waiting for transfers between devices, per_device(): lax.psum_scatter(matmul(mixed, out_rows), 'tensor', scatter_dimension=0,...  147 us
    unnamed x3, blocking collectives  141 us
    dot_general x8, matrix products, one_one_block(): jnp.einsum('hqk,qhd->khd', attn_probs.astype(jnp.bfloat16), grad_blk, pre...  134 us
    dot_general x8, matrix products, attention_one_block(): jnp.einsum('hqk,khd->qhd', attn_probs, values_slot, preferred_element_typ...  127 us
  transfers between devices with their start and end apart: 20, of which 12 were waited for; matrix products, arithmetic and copies ran while one was open for 52% of the time, Pallas kernels for 0%

commit v1 on v0

--- a/solution.py
+++ b/solution.py
@@ -1,6 +1,8 @@
 import jax
 import jax.numpy as jnp
 from jax import lax
+from jax.experimental import pallas as pl
+from jax.experimental.pallas import tpu as pltpu
 from jax.sharding import PartitionSpec as P
 
 HEAD_DIM = 64
@@ -138,7 +140,7 @@
     )
 
 
-def per_device(
+def per_device_split_heads(
     tokens,
     cotangent,
     seq_lengths,
@@ -332,6 +334,355 @@
     )
 
 
+PAIR = 2 * HEAD_DIM
+QUERY_ROWS = 512
+KEY_ROWS = 512
+LAST_DIMS = (((1,), (1,)), ((), ()))
+FIRST_DIMS = (((0,), (0,)), ((), ()))
+
+
+def dot32(left, right, dims):
+    return lax.dot_general(left, right, dims, preferred_element_type=jnp.float32)
+
+
+def lanes_of(rows):
+    return lax.broadcasted_iota(jnp.int32, (rows, PAIR), 1)
+
+
+def head_mask(rows, head):
+    first = (lanes_of(rows) < HEAD_DIM).astype(jnp.float32)
+    return first if head == 0 else 1.0 - first
+
+
+def three_parts(column, rows, lead):
+    high = column.astype(jnp.bfloat16).astype(jnp.float32)
+    rest = column - high
+    middle = rest.astype(jnp.bfloat16).astype(jnp.float32)
+    low = rest - middle
+    lane = lanes_of(rows)
+    out = jnp.where(lane == 0, lead, 0.0)
+    out = jnp.where(lane == 1, high, out)
+    out = jnp.where(lane == 2, middle, out)
+    return jnp.where(lane == 3, low, out).astype(jnp.bfloat16)
+
+
+def forward_kernel(q_ref, k_ref, v_ref, extra_ref, out_ref, lse_ref):
+    rows = q_ref.shape[0]
+    query_blk = q_ref[...] * jnp.bfloat16(HEAD_DIM**-0.5)
+    keys_wide = jnp.concatenate([k_ref[...], extra_ref[...]], axis=1)
+    one_lane = (lanes_of(rows) == 0).astype(jnp.float32).astype(jnp.bfloat16)
+    results = []
+    for head in range(2):
+        mask = head_mask(rows, head).astype(jnp.bfloat16)
+        query_wide = jnp.concatenate([query_blk * mask, one_lane], axis=1)
+        scores = dot32(query_wide, keys_wide, LAST_DIMS)
+        peak = jnp.max(scores, axis=-1, keepdims=True)
+        exponent = jnp.exp(scores - peak).astype(jnp.bfloat16)
+        own = head_mask(SEQ_MAX, head)
+        values_ones = v_ref[...] * own.astype(jnp.bfloat16) + (1.0 - own).astype(jnp.bfloat16)
+        mixed = jnp.dot(exponent, values_ones, preferred_element_type=jnp.float32)
+        summed = pltpu.roll(mixed, HEAD_DIM, 1)
+        results.append((mixed / summed, peak + jnp.log(summed)))
+    first = lanes_of(rows) < HEAD_DIM
+    out_ref[...] = jnp.where(first, results[0][0], results[1][0]).astype(jnp.bfloat16)
+    lse_ref[...] = jnp.where(first, results[0][1], results[1][1])
+
+
+def backward_kernel(
+    q_ref, k_ref, v_ref, extra_ref, grad_ref, out_ref, lse_ref, dq_ref, dk_ref, dv_ref, dk_acc, dv_acc
+):
+    rows = q_ref.shape[0]
+
+    @pl.when(pl.program_id(2) == 0)
+    def _():
+        dk_acc[...] = jnp.zeros_like(dk_acc)
+        dv_acc[...] = jnp.zeros_like(dv_acc)
+
+    query_blk = q_ref[...] * jnp.bfloat16(HEAD_DIM**-0.5)
+    product = grad_ref[...].astype(jnp.float32) * out_ref[...].astype(jnp.float32)
+    heads = []
+    for head in range(2):
+        mask = head_mask(rows, head)
+        mask_low = mask.astype(jnp.bfloat16)
+        inner = jnp.sum(product * mask, axis=-1, keepdims=True)
+        lse = lse_ref[:, head * HEAD_DIM : head * HEAD_DIM + 1]
+        query_own = query_blk * mask_low
+        grad_own = grad_ref[...] * mask_low
+        query_wide = jnp.concatenate([query_own, three_parts(-lse, rows, 1.0)], axis=1)
+        grad_wide = jnp.concatenate([grad_own, three_parts(-inner, rows, 0.0)], axis=1)
+        heads.append((query_own, grad_own, query_wide, grad_wide))
+    grad_query = jnp.zeros((PAIR, rows), jnp.float32)
+    for chunk in range(SEQ_MAX // KEY_ROWS):
+        span = pl.ds(chunk * KEY_ROWS, KEY_ROWS)
+        keys_blk = k_ref[span, :]
+        keys_wide = jnp.concatenate([keys_blk, extra_ref[span, :]], axis=1)
+        values_wide = jnp.concatenate([v_ref[span, :], extra_ref[span, :]], axis=1)
+        dk_sum = dk_acc[span, :]
+        dv_sum = dv_acc[span, :]
+        for head in range(2):
+            query_own, grad_own, query_wide, grad_wide = heads[head]
+            probs = jnp.exp(dot32(keys_wide, query_wide, LAST_DIMS))
+            grad_probs = dot32(values_wide, grad_wide, LAST_DIMS)
+            grad_scores = (probs * grad_probs).astype(jnp.bfloat16)
+            dv_sum = dv_sum + jnp.dot(
+                probs.astype(jnp.bfloat16), grad_own, preferred_element_type=jnp.float32
+            )
+            dk_sum = dk_sum + jnp.dot(grad_scores, query_own, preferred_element_type=jnp.float32)
+            keys_own = keys_blk * head_mask(KEY_ROWS, head).astype(jnp.bfloat16)
+            grad_query = grad_query + dot32(keys_own, grad_scores, FIRST_DIMS)
+        dk_acc[span, :] = dk_sum
+        dv_acc[span, :] = dv_sum
+    dq_ref[...] = (grad_query.T * HEAD_DIM**-0.5).astype(jnp.bfloat16)
+
+    @pl.when(pl.program_id(2) == pl.num_programs(2) - 1)
+    def _():
+        dk_ref[...] = dk_acc[...].astype(jnp.bfloat16)
+        dv_ref[...] = dv_acc[...].astype(jnp.bfloat16)
+
+
+def attention_specs(width):
+    pairs = width // PAIR
+    steps = SEQ_MAX // QUERY_ROWS
+
+    def row_spec(offset):
+        return pl.BlockSpec((QUERY_ROWS, PAIR), lambda s, p, i: (s * steps + i, p + offset * pairs))
+
+    def slot_spec(offset):
+        return pl.BlockSpec((SEQ_MAX, PAIR), lambda s, p, i: (s, p + offset * pairs))
+
+    extra_spec = pl.BlockSpec((SEQ_MAX, PAIR), lambda s, p, i: (s, 0))
+    return pairs, steps, row_spec, slot_spec, extra_spec
+
+
+def attention_call(qkv, extra):
+    rows, width = qkv.shape[0], qkv.shape[1] // 3
+    pairs, steps, row_spec, slot_spec, extra_spec = attention_specs(width)
+    return pl.pallas_call(
+        forward_kernel,
+        grid=(rows // SEQ_MAX, pairs, steps),
+        in_specs=[row_spec(0), slot_spec(1), slot_spec(2), extra_spec],
+        out_specs=[row_spec(0), row_spec(0)],
+        out_shape=[
+            jax.ShapeDtypeStruct((rows, width), jnp.bfloat16),
+            jax.ShapeDtypeStruct((rows, width), jnp.float32),
+        ],
+        compiler_params=pltpu.CompilerParams(vmem_limit_bytes=48 * 2**20),
+        cost_estimate=pl.CostEstimate(
+            flops=16 * rows * SEQ_MAX * width,
+            bytes_accessed=14 * rows * width,
+            transcendentals=rows * SEQ_MAX * width // HEAD_DIM,
+        ),
+    )(qkv, qkv, qkv, extra)
+
+
+def attention_pull(qkv, extra, grad_mixed, mixed, log_sums):
+    rows, width = mixed.shape
+    pairs, steps, row_spec, slot_spec, extra_spec = attention_specs(width)
+    shape = jax.ShapeDtypeStruct((rows, width), jnp.bfloat16)
+    return pl.pallas_call(
+        backward_kernel,
+        grid=(rows // SEQ_MAX, pairs, steps),
+        in_specs=[row_spec(0), slot_spec(1), slot_spec(2), extra_spec]
+        + [row_spec(0), row_spec(0), row_spec(0)],
+        out_specs=[row_spec(0), slot_spec(0), slot_spec(0)],
+        out_shape=[shape, shape, shape],
+        scratch_shapes=[pltpu.VMEM((SEQ_MAX, PAIR), jnp.float32)] * 2,
+        compiler_params=pltpu.CompilerParams(vmem_limit_bytes=48 * 2**20),
+        cost_estimate=pl.CostEstimate(
+            flops=40 * rows * SEQ_MAX * width,
+            bytes_accessed=20 * rows * width,
+            transcendentals=rows * SEQ_MAX * width // HEAD_DIM,
+        ),
+    )(qkv, qkv, qkv, extra, grad_mixed, mixed, log_sums)
+
+
+def gelu_both(pre_act):
+    size = jnp.abs(pre_act)
+    bell = jnp.exp(-0.5 * pre_act * pre_act)
+    t = 1.0 / (1.0 + (0.3275911 * 0.5**0.5) * size)
+    poly = 1.061405429
+    for coefficient in (-1.453152027, 1.421413741, -0.284496736, 0.254829592):
+        poly = poly * t + coefficient
+    tail = 0.5 * poly * t * bell
+    cdf = jnp.where(pre_act >= 0, 1.0 - tail, tail)
+    return (pre_act * cdf, cdf + pre_act * bell * 0.3989422804014327)
+
+
+def both_halves(gathered, start, size):
+    return jnp.concatenate(
+        [gathered[i, :, start : start + size] for i in range(gathered.shape[0])], axis=1
+    )
+
+
+def split_halves(whole, parts):
+    shard, width = whole.shape
+    return whole.reshape(shard, parts, width // parts)
+
+
+def per_device(
+    tokens,
+    cotangent,
+    seq_lengths,
+    slot_seq,
+    w_query,
+    w_key,
+    w_value,
+    b_query,
+    b_value,
+    w_output,
+    b_output,
+    gain_first,
+    shift_first,
+    w_up,
+    b_up,
+    w_down,
+    b_down,
+    gain_second,
+    shift_second,
+):
+    local_rows, width = tokens.shape
+    n_dp, n_tensor = lax.axis_size("dp"), lax.axis_size("tensor")
+    both = ("dp", "tensor")
+    slots = local_rows // SEQ_MAX
+    my_index = lax.axis_index("dp") * n_tensor + lax.axis_index("tensor")
+    my_slots = lax.dynamic_slice_in_dim(slot_seq, my_index * slots, slots, 0)
+    seq_ids = jnp.arange(seq_lengths.shape[0], dtype=jnp.int32)
+    lengths = jnp.sum(
+        jnp.where(my_slots[:, None] == seq_ids[None, :], seq_lengths[None, :], 0), axis=1
+    )
+    valid = jnp.arange(SEQ_MAX, dtype=jnp.int32)[None, :] < lengths[:, None]
+    key_bias = jnp.where(valid, 0.0, masked_score).reshape(-1, 1)
+    lane = jnp.arange(PAIR, dtype=jnp.int32)[None, :]
+    extra = jnp.where(
+        lane == 0, key_bias, jnp.where((lane >= 1) & (lane <= 3), 1.0, 0.0)
+    ).astype(jnp.bfloat16)
+
+    pieces = (w_query, w_key, w_value, w_output.T, w_up, w_down.T)
+    halves = lax.all_gather(jnp.concatenate(pieces, axis=1), "tensor", axis=0)
+    shards, start = [], 0
+    for piece in pieces:
+        shards.append(both_halves(halves, start, piece.shape[1]))
+        start += piece.shape[1]
+    qkv_full = lax.all_gather(jnp.concatenate(shards[:3], axis=1), "dp", axis=0, tiled=True)
+    out_t = lax.all_gather(shards[3], "dp", axis=0, tiled=True)
+    up_full = lax.all_gather(shards[4], "dp", axis=0, tiled=True)
+    down_t = lax.all_gather(shards[5], "dp", axis=0, tiled=True)
+
+    vectors = (b_output, b_down, gain_first, shift_first, gain_second, shift_second)
+    biases = (b_query, b_value, b_up)
+    small = jnp.concatenate(
+        list(vectors) + [bias.reshape(-1).astype(jnp.float32) for bias in biases]
+    )
+    small_all = lax.all_gather(small, both, axis=0)
+    each = b_output.shape[0]
+    bias_out, bias_down, gain_one, shift_one, gain_two, shift_two = [
+        small_all[:, i * each : (i + 1) * each].reshape(-1) for i in range(len(vectors))
+    ]
+    start, whole_biases = len(vectors) * each, []
+    for bias in biases:
+        block = small_all[:, start : start + bias.size]
+        block = block.reshape((n_dp, n_tensor) + bias.shape).transpose(1, 2, 0, 3)
+        whole_biases.append(block.reshape(-1))
+        start += bias.size
+    bias_query, bias_value, bias_up = whole_biases
+    bias_qkv = jnp.concatenate([bias_query, jnp.zeros_like(bias_query), bias_value])
+
+    qkv = (matmul(tokens, qkv_full) + bias_qkv).astype(jnp.bfloat16)
+    mixed, log_sums = attention_call(qkv, extra)
+    resid_one = tokens.astype(jnp.float32) + (contract_cols(mixed, out_t) + bias_out)
+    normed, normal_one, inv_one = norm_forward(resid_one, gain_one, shift_one)
+    normed_low = normed.astype(jnp.bfloat16)
+    hidden, slope = gelu_both(matmul(normed_low, up_full) + bias_up)
+    hidden, slope = hidden.astype(jnp.bfloat16), slope.astype(jnp.bfloat16)
+    resid_two = normed + (contract_cols(hidden, down_t) + bias_down)
+    layer_out, normal_two, inv_two = norm_forward(resid_two, gain_two, shift_two)
+    grad_two, grad_gain_two, grad_shift_two = norm_backward(
+        normal_two, inv_two, gain_two, cotangent.astype(jnp.float32)
+    )
+    grad_second = grad_two.astype(jnp.bfloat16)
+    grad_bias_down = jnp.sum(grad_second, axis=0, dtype=jnp.float32)
+
+    def reduce_dp(grad):
+        return lax.psum_scatter(grad.astype(jnp.bfloat16), "dp", scatter_dimension=0, tiled=True)
+
+    sum_down = reduce_dp(contract_rows(grad_second, hidden))
+    grad_pre = (matmul(grad_second, down_t) * slope.astype(jnp.float32)).astype(jnp.bfloat16)
+    sum_up = reduce_dp(contract_rows(normed_low, grad_pre))
+    grad_bias_up = jnp.sum(grad_pre, axis=0, dtype=jnp.float32)
+    grad_normed = grad_two + contract_cols(grad_pre, up_full)
+    grad_one, grad_gain_one, grad_shift_one = norm_backward(
+        normal_one, inv_one, gain_one, grad_normed
+    )
+    grad_branch = grad_one.astype(jnp.bfloat16)
+    grad_bias_out = jnp.sum(grad_branch, axis=0, dtype=jnp.float32)
+    sum_out = reduce_dp(contract_rows(grad_branch, mixed))
+    grad_mixed = matmul(grad_branch, out_t).astype(jnp.bfloat16)
+    grad_queries, grad_keys, grad_values = attention_pull(qkv, extra, grad_mixed, mixed, log_sums)
+    grad_qkv = jnp.concatenate([grad_queries, grad_keys, grad_values], axis=1)
+    sum_qkv = reduce_dp(contract_rows(tokens, grad_qkv))
+    grad_bias_query = jnp.sum(grad_queries, axis=0, dtype=jnp.float32)
+    grad_bias_value = jnp.sum(grad_values, axis=0, dtype=jnp.float32)
+    grad_tokens = grad_one + contract_cols(grad_qkv, qkv_full)
+
+    sums = [sum_qkv[:, i * width : (i + 1) * width] for i in range(3)] + [sum_out, sum_up, sum_down]
+    packed = jnp.concatenate([split_halves(total, n_tensor) for total in sums], axis=2)
+    packed = lax.psum_scatter(packed, "tensor", scatter_dimension=1, tiled=False)
+    packed = packed.astype(jnp.float32)
+    owned, start = [], 0
+    for piece in pieces:
+        owned.append(packed[:, start : start + piece.shape[1]])
+        start += piece.shape[1]
+    out_wq, out_wk, out_wv, out_wo, out_wup, out_wdown = owned
+
+    grad_vectors = (
+        grad_bias_out,
+        grad_bias_down,
+        grad_gain_one,
+        grad_shift_one,
+        grad_gain_two,
+        grad_shift_two,
+    )
+    columns = [vector.reshape(n_dp * n_tensor, each) for vector in grad_vectors]
+    for bias, grad in zip(biases, (grad_bias_query, grad_bias_value, grad_bias_up)):
+        block = grad.reshape(n_tensor, bias.shape[0], n_dp, bias.shape[1]).transpose(2, 0, 1, 3)
+        columns.append(block.reshape(n_dp * n_tensor, bias.size))
+    small_sum = lax.psum_scatter(
+        jnp.concatenate(columns, axis=1), both, scatter_dimension=0, tiled=False
+    )
+    out_bo, out_bdown, out_gain_one, out_shift_one, out_gain_two, out_shift_two = [
+        small_sum[i * each : (i + 1) * each] for i in range(len(grad_vectors))
+    ]
+    start, out_biases = len(grad_vectors) * each, []
+    for bias in biases:
+        out_biases.append(small_sum[start : start + bias.size].reshape(bias.shape))
+        start += bias.size
+    out_bq, out_bv, out_bup = out_biases
+    return (
+        layer_out,
+        grad_tokens,
+        out_wq,
+        out_wk,
+        out_wv,
+        out_bq,
+        out_bv,
+        out_wo.T,
+        out_bo,
+        out_gain_one,
+        out_shift_one,
+        out_wup,
+        out_bup,
+        out_wdown.T,
+        out_bdown,
+        out_gain_two,
+        out_shift_two,
+    )
+
+
+def choose_plan(*args):
+    plan = per_device if args[0].shape[0] % SEQ_MAX == 0 else per_device_split_heads
+    return plan(*args)
+
+
 def solution(mesh):
     in_specs = (
         P(("dp", "tensor"), None),
@@ -374,5 +725,5 @@
         P(("dp", "tensor")),
     )
     return jax.shard_map(
-        per_device, mesh=mesh, in_specs=in_specs, out_specs=out_specs, check_vma=False
-    )
+        choose_plan, mesh=mesh, in_specs=in_specs, out_specs=out_specs, check_vma=False
+    )

time: 3060 us -> 1140 us (0.37)
  matrix products: 1180 us -> 294 us
  waiting for transfers between devices: 1020 us -> 281 us
  other arithmetic: 433 us -> 33.6 us
  Pallas kernels: 0 us -> 313 us
  blocking collectives: 203 us -> 105 us
  local copies, waits for them, and re-layouts: 143 us -> 92.2 us
  loops' own time: 43.9 us -> 0 us
    dot_general x56 -> x0, matrix products: 826 us -> none  [the longest x16 309 us: masked_scores(): jnp.einsum('qhd,khd->hqk', query_blk, keys_slot, preferred_element_type=j...]
    all_gather x10 -> x5, waiting for transfers between devices: 444 us -> 30.1 us  [the longest x1 30 us: per_device(): halves = lax.all_gather(jnp.concatenate(pieces, axis=1), 'tensor', axis=0)]
    reduce_scatter x7 -> x4, waiting for transfers between devices: 571 us -> 251 us  [the longest x3 251 us: reduce_dp(): lax.psum_scatter(grad.astype(jnp.bfloat16), 'dp', scatter_dimension=0, ti...]
    pallas_call x0 -> x2, Pallas kernels: none -> 313 us  [the longest x1 189 us: attention_pull(): pl.pallas_call(backward_kernel, grid=(rows // SEQ_MAX, pairs, steps), in_...]
    convert_element_type x15 -> x2, other arithmetic: 229 us -> 1.57 us  [the longest x1 1.24 us: per_device(): packed = packed.astype(jnp.float32)]
    reduce_sum x12 -> x2, other arithmetic: 137 us -> 6.04 us  [the longest x1 3.15 us: per_device(): grad_bias_value = jnp.sum(grad_values, axis=0, dtype=jnp.float32)]
    unnamed x3 -> x1, blocking collectives: 141 us -> 37.3 us
    another operation x4 -> x0, loops' own time: 43.9 us -> none  [the longest x1 26.4 us: attention_forward(): attended, log_sums = lax.map(attention_one_block, block_ids)]
  transfers between devices with their start and end apart: 20 -> 10, of which waited for: 12 -> 4; matrix products, arithmetic and copies ran while one was open for 52% -> 20% of each run, Pallas kernels for 0% -> 11%
where the time goes in v1:
time: 1140 us
  Pallas kernels  313 us (27%)
  matrix products  294 us (26%)
  waiting for transfers between devices  281 us (25%)
  blocking collectives  105 us (9%)
  local copies, waits for them, and re-layouts  92.2 us (8%)
  other arithmetic  33.6 us (3%)
  between operations  15 us (1%)
    reduce_scatter x3, waiting for transfers between devices, reduce_dp(): lax.psum_scatter(grad.astype(jnp.bfloat16), 'dp', scatter_dimension=0, ti...  251 us
    pallas_call x1, Pallas kernels, attention_pull(): pl.pallas_call(backward_kernel, grid=(rows // SEQ_MAX, pairs, steps), in_...  189 us
    dot_general x4, matrix products, matmul(): return jnp.dot(left, right, preferred_element_type=jnp.float32)  131 us
    pallas_call x1, Pallas kernels, attention_call(): pl.pallas_call(forward_kernel, grid=(rows // SEQ_MAX, pairs, steps), in_s...  124 us
    dot_general x4, matrix products, contract_cols(): lax.dot_general(left, right, (((1,), (1,)), ((), ())), preferred_element_...  86.2 us
    dot_general x4, matrix products, contract_rows(): lax.dot_general(left, right, (((0,), (0,)), ((), ())), preferred_element_...  76.8 us
    unnamed x94, local copies, waits for them, and re-layouts  70.4 us
    all_gather x1, blocking collectives, per_device(): small_all = lax.all_gather(small, both, axis=0)  68.1 us
  transfers between devices with their start and end apart: 10, of which 4 were waited for; matrix products, arithmetic and copies ran while one was open for 20% of the time, Pallas kernels for 11%

profile of v1, /device:TPU:0, one launch (start us, length us, event | category | flops | bytes accessed | tf_op | source)
XLA Modules:
  0.0 1135.5 jit_solution(8085355256257912591)
XLA Ops:
  13.5 30.0 %all-gather.17.cloned.1.call-done = bf16[128,6144]{1,0:T(8,128)(2,1)} async-done(((bf16[64,6144]{1,0:T(8,128)(2,1)}), bf16[128,6144]{1,0:T(8,128)(2,1)}) %all-gather.17.cloned.1.call-update) | async-done | bytes 1572880 | tf_op jit(solution)/shard_map/all_gather | solution.py:561
  56.6 68.1 %all-gather.2 = f32[32,1,384]{2,1,0:T(1,128)S(1)} all-gather(f32[1,1,384]{2,1,0:T(1,128)S(1)} %reshape.253), channel_id=3, replica_groups=mesh['dp'=16,'tensor'=2] {'dp','tensor'}, dimensions={0}, use_global_device_ids=true | all-gather | bytes 50688 | tf_op jit(solution)/shard_map/all_gather | solution.py:576
  146.1 19.3 %fusion.9.q_ref.k_ref.v_ref = bf16[2048,3072]{1,0:T(8,128)(2,1)} fusion(f32[3072]{0:T(1024)S(1)} %pad_maximum_fusion.3, bf16[2048,1024]{1,0:T(8,128)(2,1)} %param.19, bf16[1024,3072]{1,0:T(8,128)(2,1)} %all-gather.9.cloned.1.call-done), kind=kOutput, calls=%fused_computation.18 | convolution fusion | flops 12897484800 | bytes 23080960 | tf_op jit(solution)/shard_map/dot_general | solution.py:17
  165.4 124.0 %shard_map.314 = (bf16[2048,1024]{1,0:T(8,128)(2,1)S(1)}, f32[2048,1024]{1,0:T(8,128)}) custom-call(bf16[2048,3072]{1,0:T(8,128)(2,1)} %fusion.9.q_ref.k_ref.v_ref, bf16[2048,3072]{1,0:T(8,128)(2,1)} %fusion.9.q_ref.k_ref.v_ref, bf16[2048,3072]{1,0:T(8,128)(2,1)} %fusion.9.q_ref.k_ref.v_ref, bf16[2048,128]{1,0:T(8,128)(2,1)S(1)} %select_convert_fusion.extra_ref), custom_call_target="tpu_custom_call" | custom-call | flops 68719476736 | bytes 29360128 | tf_op jit(solution)/shard_map/pallas_call | solution.py:460
  291.4 8.7 fusion.32
  304.4 50.9 %multiply_convert_fusion.1 = (bf16[2048,4096]{1,0:T(8,128)(2,1)}, f32[2048,4096]{1,0:T(8,128)}) fusion(f32[4096]{0:T(1024)S(1)} %add.147, bf16[1024,4096]{1,0:T(8,128)(2,1)} %all-gather.13.cloned.1.call-done, f32[2048,1024]{0,1:T(8,128)} %copy-done.3, f32[1024]{0:T(1024)S(1)} %add.144, f32[1024]{0:T(1024)S(1)} %mul.158, f32[2048]{0:T(1024)S(1)} %add_rsqrt_fusion.1, ...), kind=kOutput, calls=%fused_computation.10 | convolution fusion | flops 17383292928 | bytes 67149824 | tf_op jit(solution)/shard_map/dot_general | solution.py:17
  355.4 24.5 %fusion.33 = (f32[2048]{0:T(1024)S(1)}, f32[2048,1024]{0,1:T(8,128)S(1)}) fusion(f32[1024]{0:T(1024)S(1)} %copy-done.28, bf16[2048,4096]{1,0:T(8,128)(2,1)} %get-tuple-element.126, bf16[1024,4096]{1,0:T(8,128)(2,1)} %all-gather.15.cloned.1.call-done, f32[1024]{0:T(1024)S(1)} %add.144, f32[1024]{0:T(1024)S(1)} %mul.158, f32[2048]{0:T(1024)S(1)} %add_rsqrt_fusion.1, ...), kind=kOutput, calls=%fused_computation.119 | convolution fusion | flops 17194547200 | bytes 41979904 | tf_op jit(solution)/shard_map/dot_general | solution.py:27
  386.6 7.3 convert_reduce_fusion.4
  393.9 54.3 %convert_reduce_fusion = (f32[4096]{0:T(1024)}, bf16[2048,4096]{1,0:T(8,128)(2,1)}) fusion(f32[2048,4096]{1,0:T(8,128)} %get-tuple-element.127, f32[4096]{0:T(1024)S(1)} %add.147, bf16[2048,1024]{0,1:T(8,128)(2,1)} %get-tuple-element.89, bf16[1024,4096]{1,0:T(8,128)(2,1)} %all-gather.15.cloned.1.call-done), kind=kOutput, calls=%fused_computation.8 | convolution fusion | flops 17431523328 | bytes 62947328 | tf_op jit(solution)/shard_map/dot_general | solution.py:17
  448.1 31.8 %multiply_reduce_fusion = (f32[1024]{0:T(1024)}, f32[2048]{0:T(1024)S(1)}, f32[2048]{0:T(1024)S(1)}, f32[1024]{0:T(1024)}, f32[2048,1024]{0,1:T(8,128)}) fusion(f32[2048,1024]{0,1:T(8,128)} %copy-done.3, f32[2048]{0:T(1024)S(1)} %add_rsqrt_fusion.1, f32[2048]{0:T(1024)S(1)} %broadcast_multiply_fusion.5, f32[1024]{0:T(1024)S(1)} %mul.158, ...), kind=kOutput, calls=%fused_computation.25 | convolution fusion | flops 17217613824 | bytes 54607872 | tf_op jit(solution)/shard_map/dot_general | solution.py:27
  480.0 8.1 convert_reduce_fusion.5
  494.3 189.0 %shard_map.315 = (bf16[2048,1024]{1,0:T(8,128)(2,1)S(1)}, bf16[2048,1024]{1,0:T(8,128)(2,1)}, bf16[2048,1024]{1,0:T(8,128)(2,1)}) custom-call(bf16[2048,3072]{1,0:T(8,128)(2,1)} %fusion.9.q_ref.k_ref.v_ref, bf16[2048,3072]{1,0:T(8,128)(2,1)} %fusion.9.q_ref.k_ref.v_ref, bf16[2048,3072]{1,0:T(8,128)(2,1)} %fusion.9.q_ref.k_ref.v_ref, ...), custom_call_target="tpu_custom_call" | custom-call | flops 171798691840 | bytes 41943040 | tf_op jit(solution)/shard_map/pallas_call | solution.py:482
  693.6 17.5 %convert_bitcast_fusion = bf16[1024,3072]{0,1:T(8,128)(2,1)} fusion(bf16[2048,3072]{1,0:T(8,128)(2,1)} %constant_dynamic-update-slice_fusion.4, bf16[2048,1024]{1,0:T(8,128)(2,1)S(1)} %copy-done.6), kind=kOutput, calls=%fused_computation.42 | convolution fusion | flops 12888047616 | bytes 23068672 | tf_op jit(solution)/shard_map/dot_general | solution.py:21
  711.1 8.6 copy.112
  720.0 11.2 convolution_convert_fusion.3
  731.3 25.2 %convolution_convert_fusion.1 = bf16[1024,4096]{1,0:T(8,128)(2,1)} fusion(bf16[2048,4096]{1,0:T(8,128)(2,1)} %get-tuple-element.132, f32[2048,1024]{0,1:T(8,128)} %copy-done.3, f32[1024]{0:T(1024)S(1)} %copy-done.25, f32[1024]{0:T(1024)S(1)} %copy-done.19, f32[2048]{0:T(1024)S(1)} %copy-done.15, f32[2048]{0:T(1024)S(1)} %copy-done.12), kind=kOutput, calls=%fused_computation.39 | convolution fusion | flops 17194549248 | bytes 33579008 | tf_op jit(solution)/shard_map/dot_general | solution.py:21
  756.6 22.9 %convolution_convert_fusion = bf16[1024,4096]{1,0:T(8,128)(2,1)} fusion(bf16[2048,1024]{0,1:T(8,128)(2,1)} %get-tuple-element.89, bf16[2048,4096]{1,0:T(8,128)(2,1)} %get-tuple-element.126), kind=kOutput, calls=%fused_computation.38 | convolution fusion | flops 17184063488 | bytes 29360128 | tf_op jit(solution)/shard_map/dot_general | solution.py:21
  788.0 37.3 %all-reduce = f32[32,384]{1,0:T(8,128)S(1)} all-reduce(f32[32,384]{1,0:T(8,128)S(1)} %concatenate.39), channel_id=9, replica_groups=mesh['dp'=16,'tensor'=2] {'dp','tensor'}, use_global_device_ids=true, to_apply=%region_23.24.clone | all-reduce | flops 12288 | bytes 98304
  830.3 35.8 %reduce-scatter.8.cloned.1.call-done = bf16[64,1024]{1,0:T(8,128)(2,1)} async-done(((bf16[1024,1024]{1,0:T(8,128)(2,1)}), bf16[64,1024]{1,0:T(8,128)(2,1)}) %reduce-scatter.8.cloned.1.call-update) | async-done | bytes 131088 | tf_op jit(solution)/shard_map/reduce_scatter | solution.py:606
  867.0 107.3 %reduce-scatter.10.cloned.1.call-done = bf16[64,4096]{1,0:T(8,128)(2,1)} async-done(((bf16[1024,4096]{1,0:T(8,128)(2,1)}), bf16[64,4096]{1,0:T(8,128)(2,1)}) %reduce-scatter.10.cloned.1.call-update) | async-done | bytes 524304 | tf_op jit(solution)/shard_map/reduce_scatter | solution.py:606
  975.4 108.0 %reduce-scatter.12.cloned.1.call-done = bf16[64,4096]{1,0:T(8,128)(2,1)} async-done(((bf16[1024,4096]{1,0:T(8,128)(2,1)}), bf16[64,4096]{1,0:T(8,128)(2,1)}) %reduce-scatter.12.cloned.1.call-update) | async-done | bytes 524304 | tf_op jit(solution)/shard_map/reduce_scatter | solution.py:606
  1085.6 21.2 %convolution_add_fusion.1 = f32[2048,1024]{0,1:T(8,128)} fusion(f32[2048,1024]{0,1:T(8,128)} %copy-done.5, bf16[2048,3072]{1,0:T(8,128)(2,1)} %constant_dynamic-update-slice_fusion.4, bf16[1024,3072]{1,0:T(8,128)(2,1)} %all-gather.9.cloned.1.call-done), kind=kOutput, calls=%fused_computation.44 | convolution fusion | flops 12886999040 | bytes 35651584 | tf_op jit(solution)/shard_map/dot_general | solution.py:27
  1106.8 9.3 copy.104
  1116.1 9.2 copy.103
  (199 shorter events, 90.9 us)
Async XLA Ops:
  7.2 36.3 %all-gather.17.cloned.1.call-start = ((), (), s32[]{:S(2)}) async-start(), calls=%async_computation.13 | async-start | bytes 2359296 | tf_op jit(solution)/shard_map/all_gather | solution.py:561
  13.5 132.6 %all-gather.9.cloned.1.call-start = ((), (), s32[]{:S(2)}) async-start(), calls=%async_computation.5 | async-start | bytes 6684672 | tf_op jit(solution)/shard_map/all_gather | solution.py:566
  49.4 242.0 %all-gather.11.cloned.1.call-start = ((), (), s32[]{:S(2)}) async-start(), calls=%async_computation.6 | async-start | bytes 2228224 | tf_op jit(solution)/shard_map/all_gather | solution.py:567
  51.0 253.4 %all-gather.13.cloned.1.call-start = ((), (), s32[]{:S(2)}) async-start(), calls=%async_computation.7 | async-start | bytes 8912896 | tf_op jit(solution)/shard_map/all_gather | solution.py:568
  53.2 302.2 %all-gather.15.cloned.1.call-start = ((), (), s32[]{:S(2)}) async-start(), calls=%async_computation.8 | async-start | bytes 8912896 | tf_op jit(solution)/shard_map/all_gather | solution.py:569
  125.5 16.3 %copy-start.30 = (s32[32]{0:T(128)S(1)}, s32[32]{0:T(128)}, u32[]{:S(2)}) copy-start(s32[32]{0:T(128)} %param.22) | copy-start | bytes 388
  125.5 16.8 %copy-start.31 = (s32[32]{0:T(128)S(1)}, s32[32]{0:T(128)}, u32[]{:S(2)}) copy-start(s32[32]{0:T(128)} %param.21) | copy-start | bytes 388
  132.0 347.9 %copy-start.18 = (f32[1024]{0:T(1024)}, f32[1024]{0:T(1024)S(1)}, u32[]{:S(2)}) copy-start(f32[1024]{0:T(1024)S(1)} %mul.158) | copy-start | bytes 12292
  132.1 223.2 %copy-start.24 = (f32[1024]{0:T(1024)}, f32[1024]{0:T(1024)S(1)}, u32[]{:S(2)}) copy-start(f32[1024]{0:T(1024)S(1)} %add.144) | copy-start | bytes 12292
  145.5 682.7 %reduce-scatter.16.cloned.1.call-start = ((), (), s32[]{:S(2)}) async-start(), calls=%async_computation.14 | async-start | bytes 6684672
  300.1 179.8 %copy-start.11 = (f32[2048]{0:T(1024)}, f32[2048]{0:T(1024)S(1)}, u32[]{:S(2)}) copy-start(f32[2048]{0:T(1024)S(1)} %broadcast_multiply_fusion.5) | copy-start | bytes 24580
  304.4 175.6 %copy-start.14 = (f32[2048]{0:T(1024)}, f32[2048]{0:T(1024)S(1)}, u32[]{:S(2)}) copy-start(f32[2048]{0:T(1024)S(1)} %add_rsqrt_fusion.1) | copy-start | bytes 24580
  304.4 51.0 %copy-start.28 = (f32[1024]{0:T(1024)S(1)}, f32[1024]{0:T(1024)}, u32[]{:S(2)}) copy-start(f32[1024]{0:T(1024)} %add.159) | copy-start | bytes 12292
  719.7 11.5 %copy-start.12 = (f32[2048]{0:T(1024)S(1)}, f32[2048]{0:T(1024)}, u32[]{:S(2)}) copy-start(f32[2048]{0:T(1024)} %copy-done.11) | copy-start | bytes 24580
  719.7 11.5 %copy-start.15 = (f32[2048]{0:T(1024)S(1)}, f32[2048]{0:T(1024)}, u32[]{:S(2)}) copy-start(f32[2048]{0:T(1024)} %copy-done.14) | copy-start | bytes 24580
  719.7 11.5 %copy-start.19 = (f32[1024]{0:T(1024)S(1)}, f32[1024]{0:T(1024)}, u32[]{:S(2)}) copy-start(f32[1024]{0:T(1024)} %copy-done.18) | copy-start | bytes 12292
  719.7 11.5 %copy-start.25 = (f32[1024]{0:T(1024)S(1)}, f32[1024]{0:T(1024)}, u32[]{:S(2)}) copy-start(f32[1024]{0:T(1024)} %copy-done.24) | copy-start | bytes 12292
  719.7 146.3 %reduce-scatter.8.cloned.1.call-start = ((), (), s32[]{:S(2)}) async-start(), calls=%async_computation.9 | async-start | bytes 2228224 | tf_op jit(solution)/shard_map/reduce_scatter | solution.py:606
  731.2 243.1 %reduce-scatter.10.cloned.1.call-start = ((), (), s32[]{:S(2)}) async-start(), calls=%async_computation.10 | async-start | bytes 8912896 | tf_op jit(solution)/shard_map/reduce_scatter | solution.py:606
  756.5 326.8 %reduce-scatter.12.cloned.1.call-start = ((), (), s32[]{:S(2)}) async-start(), calls=%async_computation.11 | async-start | bytes 8912896 | tf_op jit(solution)/shard_map/reduce_scatter | solution.py:606
  779.4 8.2 copy-start.20
  779.5 8.3 copy-start.17
  779.5 8.3 copy-start.16
  779.5 345.9 %reduce-scatter.14.cloned.1.call-start = ((), (), s32[]{:S(2)}) async-start(), calls=%async_computation.12 | async-start | bytes 2359296 | tf_op jit(solution)/shard_map/reduce_scatter | solution.py:629
  (18 other events, 86.7 us)
Sparse Core Ops, SparseCore 0:
  13.6 29.8 all-gather.16
  49.5 62.0 all-gather.8
  114.3 40.0 all-gather.10
  157.0 73.6 all-gather.12
  233.2 73.1 all-gather.14
  719.8 81.3 reduce-scatter.15
  805.4 60.6 reduce-scatter.7
  870.7 103.5 reduce-scatter.9
  978.9 104.3 reduce-scatter.11
  1085.7 25.8 reduce-scatter.13
